TPU v7x, 32 devices: a whole 2x2x4 slice. The times are simulated.
32 devices in a mesh: groups: 2 (over x), seq: 16 (over z, y, core).
Axes of the slice: x: 2, y: 2, z: 4, core: 2. Of those that a mesh axis runs over, the one named last changes fastest.
Arguments:
- queries: bfloat16 [12288, 2048], P(('groups', 'seq')), parts along dimension 0, may hold values from -6 to 6
- keys: bfloat16 [12288, 2048], P(('groups', 'seq')), parts along dimension 0, may hold values from -6 to 6
- values: bfloat16 [12288, 2048], P(('groups', 'seq')), parts along dimension 0, may hold values from -6 to 6
- out_grad: bfloat16 [12288, 2048], P(('groups', 'seq')), parts along dimension 0, may hold values from -6 to 6
Outputs:
- relaid: bfloat16 [16, 12288, 128], P('seq', 'groups'), parts along dimension 1
- query_grad: bfloat16 [12288, 2048], P(('groups', 'seq')), parts along dimension 0
- key_grad: bfloat16 [12288, 2048], P(('groups', 'seq')), parts along dimension 0
- value_grad: bfloat16 [12288, 2048], P(('groups', 'seq')), parts along dimension 0
There are 2 independent parts, one for each index of `groups`. A program takes and returns all parts, laid end to end along the dimension named above; each array names one. Nothing has to cross between parts.
All inputs are finite; a program needn't handle non-finite values.
Results may differ from a plain program's by a relative error of at most 0.0058.
Values may be sent and summed in bfloat16 or wider, within the bound.
A program may use at most 128 MiB of HBM per device.

v0:
```python
import jax
import jax.numpy as jnp
from jax import lax
from jax.sharding import PartitionSpec as P

DH = 128


eps = 1e-06


def blocks_before(columns, earlier):
    count = columns.shape[0]
    row_ids = lax.broadcasted_iota(jnp.int32, (count, count), 0)
    col_ids = lax.broadcasted_iota(jnp.int32, (count, count), 1)
    if earlier:
        select = (col_ids < row_ids).astype(jnp.float32)
    else:
        select = (col_ids > row_ids).astype(jnp.float32)
    summed = jnp.dot(
        select, columns, precision=lax.Precision.HIGHEST, preferred_element_type=jnp.float32
    )
    return summed


def earlier_sum(local):
    flat = local.reshape(1, -1)
    columns = lax.all_to_all(flat, "seq", split_axis=1, concat_axis=0, tiled=True)
    shifted = blocks_before(columns, True)
    merged = lax.all_to_all(
        shifted.astype(jnp.bfloat16), "seq", split_axis=0, concat_axis=1, tiled=True
    ).astype(shifted.dtype)
    return merged.reshape(local.shape)


def later_sum(local):
    flat = local.reshape(1, -1)
    columns = lax.all_to_all(flat, "seq", split_axis=1, concat_axis=0, tiled=True)
    shifted = blocks_before(columns, False)
    merged = lax.all_to_all(
        shifted.astype(jnp.bfloat16), "seq", split_axis=0, concat_axis=1, tiled=True
    ).astype(shifted.dtype)
    return merged.reshape(local.shape)


def body(queries, keys, values, out_grad):
    rows = queries.shape[0]
    width = queries.shape[1]
    heads = width // DH
    f32 = jnp.float32
    q3 = queries.reshape(rows, heads, DH)
    k3 = keys.reshape(rows, heads, DH)
    v3 = values.reshape(rows, heads, DH)
    row_ids = lax.broadcasted_iota(jnp.int32, (rows, rows), 0)
    col_ids = lax.broadcasted_iota(jnp.int32, (rows, rows), 1)
    causal = (row_ids >= col_ids)[None]
    local_state = jnp.einsum("shd,she->hde", k3, v3, preferred_element_type=f32)
    scores = jnp.einsum("thd,shd->hts", q3, k3, preferred_element_type=f32)
    masked = jnp.where(causal, scores, 0.0).astype(jnp.bfloat16)
    intra = jnp.einsum("hts,shd->thd", masked, v3, preferred_element_type=f32)
    prefix_b = earlier_sum(local_state).astype(jnp.bfloat16)
    inter = jnp.einsum("thd,hde->the", q3, prefix_b, preferred_element_type=f32)
    acc = intra + inter
    norm = jnp.sqrt(jnp.mean(acc * acc, axis=-1, keepdims=True) + eps)
    unit = acc / norm
    out_heads = unit.astype(jnp.bfloat16)
    splits = lax.axis_size("seq") // heads
    piece_rows = rows // splits
    outgoing = out_heads.reshape(splits, piece_rows, heads, DH)
    outgoing = jnp.transpose(outgoing, (0, 2, 1, 3)).reshape(splits * heads, piece_rows, DH)
    relaid = lax.all_to_all(outgoing, "seq", split_axis=0, concat_axis=1, tiled=True)
    grad_rows = out_grad.reshape(rows, heads, DH).astype(f32)
    inner = jnp.mean(grad_rows * unit, axis=-1, keepdims=True)
    d_acc = ((grad_rows - unit * inner) / norm).astype(jnp.bfloat16)
    back_state = jnp.einsum("thd,the->hde", q3, d_acc, preferred_element_type=f32)
    later_b = later_sum(back_state).astype(jnp.bfloat16)
    dscore = jnp.einsum("thd,shd->hts", d_acc, v3, preferred_element_type=f32)
    dscore = jnp.where(causal, dscore, 0.0).astype(jnp.bfloat16)
    query_grad = jnp.einsum("hts,shd->thd", dscore, k3, preferred_element_type=f32)
    query_grad = query_grad + jnp.einsum(
        "the,hde->thd", d_acc, prefix_b, preferred_element_type=f32
    )
    key_grad = jnp.einsum("hts,thd->shd", dscore, q3, preferred_element_type=f32)
    key_grad = key_grad + jnp.einsum("she,hde->shd", v3, later_b, preferred_element_type=f32)
    value_grad = jnp.einsum("hts,the->she", masked, d_acc, preferred_element_type=f32)
    value_grad = value_grad + jnp.einsum("shd,hde->she", k3, later_b, preferred_element_type=f32)
    return (
        relaid,
        query_grad.astype(jnp.bfloat16).reshape(rows, width),
        key_grad.astype(jnp.bfloat16).reshape(rows, width),
        value_grad.astype(jnp.bfloat16).reshape(rows, width),
    )


def solution(mesh):
    return jax.shard_map(
        body,
        mesh=mesh,
        in_specs=(
            P(("groups", "seq"), None),
            P(("groups", "seq"), None),
            P(("groups", "seq"), None),
            P(("groups", "seq"), None),
        ),
        out_specs=(
            P("seq", "groups", None),
            P(("groups", "seq"), None),
            P(("groups", "seq"), None),
            P(("groups", "seq"), None),
        ),
        check_vma=False,
    )
```

profile of v0, /device:TPU:0, one launch (start us, length us, event | category | flops | bytes accessed | tf_op | source)
XLA Modules:
  0.0 182.9 jit_solution(17124694191122851817)
XLA Ops:
  0.6 3.1 %copy.111 = bf16[48,8,16,128]{3,2,1,0:T(8,128)(2,1)} copy(bf16[48,8,16,128]{3,1,2,0:T(8,128)(2,1)} %bitcast.126) | data formatting | bytes 3145728
  3.7 2.1 %copy.79 = bf16[384,16,128]{0,2,1:T(8,128)(2,1)S(1)} copy(bf16[384,16,128]{2,1,0:T(8,128)(2,1)} %bitcast.125) | data formatting | bytes 3145728 | tf_op jit(solution)/shard_map/reshape | solution.py:52
  7.0 32.0 %all_to_all.76 = f32[1,16,16384]{2,0,1:T(1,128)S(1)} all-to-all(f32[1,16,16384]{2,0,1:T(1,128)S(1)} %bitcast.135), channel_id=1, replica_groups=mesh['groups'=2,'seq'=16] {'seq'}, dimensions={1} | all-to-all | bytes 2097152 | tf_op jit(solution)/shard_map/all_to_all | solution.py:28
  42.9 5.1 %all-to-all-start.1 = ((bf16[16,2,8192]{2,1,0:T(2,128)(2,1)}), bf16[16,2,8192]{2,1,0:T(2,128)(2,1)}, u32[]{:S(2)}, u32[]{:S(2)}) async-start(bf16[16,2,8192]{2,1,0:T(2,128)(2,1)} %reshape.106), calls=%async_computation.1 | async-start | bytes 1048576 | tf_op jit(solution)/shard_map/all_to_all | solution.py:30
  48.0 3.2 %copy.86 = f32[384,2048]{0,1:T(8,128)} copy(bf16[384,2048]{1,0:T(8,128)(2,1)} %param.7) | data formatting | bytes 4718592 | tf_op jit(solution)/shard_map/convert_element_type | solution.py:72
  51.2 4.9 %select_convert_fusion.1 = bf16[16,384,384]{2,1,0:T(8,128)(2,1)} fusion(pred[384,384]{1,0:T(8,128)(4,1)S(1)} %iota_compare_fusion, bf16[384,2048]{1,0:T(8,128)(2,1)} %param.5, bf16[384,2048]{1,0:T(8,128)(2,1)S(1)} %copy-done.6), kind=kOutput, calls=%fused_computation.5 | convolution fusion | flops 608698368 | bytes 8011776 | tf_op jit(solution)/shard_map/thd,shd->hts/dot_general | solution.py:58
  56.2 6.3 %all-to-all-done.1 = bf16[16,2,8192]{2,1,0:T(2,128)(2,1)} async-done(((bf16[16,2,8192]{2,1,0:T(2,128)(2,1)}), bf16[16,2,8192]{2,1,0:T(2,128)(2,1)}, u32[]{:S(2)}, u32[]{:S(2)}) %all-to-all-start.1) | async-done | bytes 524320 | tf_op jit(solution)/shard_map/all_to_all | solution.py:30
  62.5 3.5 %reshape.107 = bf16[16,1,16384]{2,1,0:T(2,128)(2,1)} reshape(bf16[16,2,8192]{2,1,0:T(2,128)(2,1)} %all-to-all-done.1) | data formatting | bytes 1048576
  65.9 5.1 %reduce = bf16[16,16384]{1,0:T(8,128)(2,1)} reduce(bf16[16,1,16384]{2,1,0:T(2,128)(2,1)} %reshape.107, bf16[]{:T(256)} %constant.8), dimensions={1}, to_apply=%all_to_all.61.reduce_sub_computation | reduce | bytes 1048578 | tf_op jit(solution)/shard_map/all_to_all | solution.py:30
  80.8 2.5 %copy.93 = f32[16,128,128]{2,1,0:T(8,128)} copy(f32[16,128,128]{1,2,0:T(8,128)} %fusion.20) | data formatting | bytes 2097152 | tf_op jit(solution)/shard_map/thd,the->hde/dot_general | solution.py:75
  83.3 28.9 %all_to_all.77 = f32[1,16,16384]{2,0,1:T(1,128)S(1)} all-to-all(f32[1,16,16384]{2,0,1:T(1,128)} %bitcast.134), channel_id=1, replica_groups=mesh['groups'=2,'seq'=16] {'seq'}, dimensions={1} | all-to-all | bytes 2097152 | tf_op jit(solution)/shard_map/all_to_all | solution.py:38
  114.2 2.6 %reduce.3 = bf16[16,16384]{1,0:T(8,128)(2,1)} reduce(bf16[16,1,16384]{2,0,1:T(8,128)(2,1)} %fusion.1, bf16[]{:T(256)} %broadcast.25), dimensions={1}, to_apply=%copy.95.reduce_sub_computation | reduce | bytes 1048578 | tf_op jit(solution)/shard_map/all_to_all | solution.py:40
  116.9 2.2 %reshape.108 = bf16[16,2,8192]{2,1,0:T(2,128)(2,1)} reshape(bf16[16,16384]{1,0:T(8,128)(2,1)} %reduce.3) | data formatting | bytes 1048576
  119.1 19.6 %all_to_all.78 = bf16[16,2,8192]{2,1,0:T(2,128)(2,1)} all-to-all(bf16[16,2,8192]{2,1,0:T(2,128)(2,1)} %reshape.108), channel_id=1, replica_groups=mesh['groups'=2,'seq'=16] {'seq'}, dimensions={0} | all-to-all | bytes 1048576 | tf_op jit(solution)/shard_map/all_to_all | solution.py:40
  138.7 4.6 %all-to-all-start.2 = ((bf16[16,384,128]{1,2,0:T(8,128)(2,1)}), bf16[16,384,128]{1,2,0:T(8,128)(2,1)}, u32[]{:S(2)}, u32[]{:S(2)}) async-start(bf16[16,384,128]{1,2,0:T(8,128)(2,1)} %get-tuple-element.21), calls=%async_computation.2 | async-start | bytes 3145728 | tf_op jit(solution)/shard_map/all_to_all | solution.py:71
  146.6 2.7 %fusion.3 = bf16[384,16,128]{0,2,1:T(8,128)(2,1)} fusion(f32[16,128,384]{2,1,0:T(8,128)S(1)} %fusion.35, bf16[16,384,384]{2,1,0:T(8,128)(2,1)S(1)} %select_convert_fusion, bf16[384,16,128]{0,2,1:T(8,128)(2,1)S(1)} %copy-done.5), kind=kOutput, calls=%fused_computation.9 | convolution fusion | flops 605552640 | bytes 11010048 | tf_op jit(solution)/shard_map/hts,shd->thd/dot_general | solution.py:79
  149.3 2.6 %copy.99 = bf16[384,2048]{1,0:T(8,128)(2,1)} copy(bf16[384,2048]{0,1:T(8,128)(2,1)} %bitcast.127) | data formatting | bytes 3145728
  151.9 5.2 %fusion.36 = f32[16,128,384]{2,1,0:T(8,128)} fusion(bf16[384,16,128]{0,2,1:T(8,128)(2,1)S(1)} %get-tuple-element.20, bf16[16,384,384]{2,1,0:T(8,128)(2,1)} %select_convert_fusion.1), kind=kOutput, calls=%fused_computation.52 | convolution fusion | flops 603979776 | bytes 9437184 | tf_op jit(solution)/shard_map/hts,the->she/dot_general | solution.py:85
  157.1 3.5 %reshape.109 = bf16[16,1,16384]{2,1,0:T(2,128)(2,1)} reshape(bf16[16,2,8192]{2,1,0:T(2,128)(2,1)} %all_to_all.78) | data formatting | bytes 1048576
  160.6 5.2 %reduce.1 = bf16[16,16384]{1,0:T(8,128)(2,1)} reduce(bf16[16,1,16384]{2,1,0:T(2,128)(2,1)} %reshape.109, bf16[]{:T(256)} %constant.8), dimensions={1}, to_apply=%all_to_all.69.reduce_sub_computation | reduce | bytes 1048578 | tf_op jit(solution)/shard_map/all_to_all | solution.py:40
  166.9 4.0 %add_convert_fusion = bf16[16,128,384]{2,1,0:T(8,128)(2,1)} fusion(f32[16,128,384]{2,1,0:T(8,128)} %fusion.36, bf16[16,128,128]{2,1,0:T(8,128)(2,1)S(1)} %bitcast.132, bf16[384,2048]{1,0:T(8,128)(2,1)S(1)} %copy-done.9), kind=kOutput, calls=%fused_computation.11 | convolution fusion | flops 202899456 | bytes 6815744 | tf_op jit(solution)/shard_map/shd,hde->she/dot_general | solution.py:86
  170.9 2.6 %copy.101 = bf16[384,2048]{1,0:T(8,128)(2,1)} copy(bf16[384,2048]{0,1:T(8,128)(2,1)} %bitcast.129) | data formatting | bytes 3145728
  175.0 3.7 %fusion.2 = bf16[384,16,128]{0,2,1:T(8,128)(2,1)S(1)} fusion(f32[16,128,384]{2,1,0:T(8,128)S(1)} %fusion.5, bf16[16,384,384]{2,1,0:T(8,128)(2,1)} %copy-done.3, bf16[384,2048]{1,0:T(8,128)(2,1)S(1)} %copy-done.8), kind=kOutput, calls=%fused_computation.7 | convolution fusion | flops 605552640 | bytes 11010048 | tf_op jit(solution)/shard_map/hts,thd->shd/dot_general | solution.py:83
  180.3 2.6 %copy.85 = bf16[16,384,128]{2,1,0:T(8,128)(2,1)} copy(bf16[16,384,128]{1,2,0:T(8,128)(2,1)} %all-to-all-done.2) | data formatting | bytes 3145728 | tf_op jit(solution)/shard_map/all_to_all | solution.py:71
  (47 shorter events, 24.2 us)
Async XLA Ops:
  0.6 5.2 %copy-start = (bf16[384,2048]{1,0:T(8,128)(2,1)S(1)}, bf16[384,2048]{1,0:T(8,128)(2,1)}, u32[]{:S(2)}) copy-start(bf16[384,2048]{1,0:T(8,128)(2,1)} %param.6) | copy-start | bytes 4718596
  5.9 1.1 copy-start.4
  42.9 19.6 %all-to-all-start.1 = ((bf16[16,2,8192]{2,1,0:T(2,128)(2,1)}), bf16[16,2,8192]{2,1,0:T(2,128)(2,1)}, u32[]{:S(2)}, u32[]{:S(2)}) async-start(bf16[16,2,8192]{2,1,0:T(2,128)(2,1)} %reshape.106), calls=%async_computation.1 | async-start | bytes 1048576 | tf_op jit(solution)/shard_map/all_to_all | solution.py:30
  48.0 3.3 %copy-start.6 = (bf16[384,2048]{1,0:T(8,128)(2,1)S(1)}, bf16[384,2048]{1,0:T(8,128)(2,1)}, u32[]{:S(2)}) copy-start(bf16[384,2048]{1,0:T(8,128)(2,1)} %param.4) | copy-start | bytes 4718596
  72.1 0.8 copy-start.10
  72.2 2.5 %copy-start.2 = (bf16[16,384,384]{2,1,0:T(8,128)(2,1)S(1)}, bf16[16,384,384]{2,1,0:T(8,128)(2,1)}, u32[]{:S(2)}) copy-start(bf16[16,384,384]{2,1,0:T(8,128)(2,1)} %select_convert_fusion.1) | copy-start | bytes 14155780
  74.7 1.9 %copy-start.1 = (f32[384,2048]{0,1:T(8,128)S(1)}, f32[384,2048]{0,1:T(8,128)}, u32[]{:S(2)}) copy-start(f32[384,2048]{0,1:T(8,128)} %copy.86) | copy-start | bytes 9437188
  77.2 2.0 %copy-start.7 = (bf16[384,2048]{1,0:T(8,128)(2,1)S(1)}, bf16[384,2048]{1,0:T(8,128)(2,1)}, u32[]{:S(2)}) copy-start(bf16[384,2048]{1,0:T(8,128)(2,1)} %param.4) | copy-start | bytes 4718596
  138.7 41.7 %all-to-all-start.2 = ((bf16[16,384,128]{1,2,0:T(8,128)(2,1)}), bf16[16,384,128]{1,2,0:T(8,128)(2,1)}, u32[]{:S(2)}, u32[]{:S(2)}) async-start(bf16[16,384,128]{1,2,0:T(8,128)(2,1)} %get-tuple-element.21), calls=%async_computation.2 | async-start | bytes 3145728 | tf_op jit(solution)/shard_map/all_to_all | solution.py:71
  144.9 1.7 copy-start.5
  146.6 2.7 %copy-start.3 = (bf16[16,384,384]{2,1,0:T(8,128)(2,1)}, bf16[16,384,384]{2,1,0:T(8,128)(2,1)S(1)}, u32[]{:S(2)}) copy-start(bf16[16,384,384]{2,1,0:T(8,128)(2,1)S(1)} %select_convert_fusion) | copy-start | bytes 14155780
  160.6 6.3 %copy-start.9 = (bf16[384,2048]{1,0:T(8,128)(2,1)S(1)}, bf16[384,2048]{1,0:T(8,128)(2,1)}, u32[]{:S(2)}) copy-start(bf16[384,2048]{1,0:T(8,128)(2,1)} %param.5) | copy-start | bytes 4718596
  166.9 4.1 %copy-start.11 = (bf16[2,8,128,128]{3,2,1,0:T(8,128)(2,1)}, bf16[2,8,128,128]{3,2,1,0:T(8,128)(2,1)S(1)}, u32[]{:S(2)}) copy-start(bf16[2,8,128,128]{3,2,1,0:T(8,128)(2,1)S(1)} %copy.113) | copy-start | bytes 1572868
  170.9 2.6 %copy-start.12 = (bf16[2,8,128,128]{3,2,1,0:T(8,128)(2,1)S(1)}, bf16[2,8,128,128]{3,2,1,0:T(8,128)(2,1)}, u32[]{:S(2)}) copy-start(bf16[2,8,128,128]{3,2,1,0:T(8,128)(2,1)} %copy-done.11) | copy-start | bytes 1572868
  173.6 1.4 copy-start.8
where the time goes:
time: 184 us; the launch traced here: 183 us
  blocking collectives  80.5 us (44%)
  local copies, waits for them, and re-layouts  36.6 us (20%)
  matrix products  32.4 us (18%)
  other arithmetic  16.5 us (9%)
  starting transfers between devices  9.68 us (5%)
  waiting for transfers between devices  6.29 us (3%)
    all_to_all x1, blocking collectives, earlier_sum(): lax.all_to_all(flat, 'seq', split_axis=1, concat_axis=0, tiled=True)  32 us
    all_to_all x1, blocking collectives, later_sum(): lax.all_to_all(flat, 'seq', split_axis=1, concat_axis=0, tiled=True)  28.9 us
    unnamed x36, local copies, waits for them, and re-layouts  25.7 us
    all_to_all x1, blocking collectives, later_sum(): lax.all_to_all(shifted.astype(jnp.bfloat16), 'seq', split_axis=0, concat_...  19.6 us
    all_to_all x2, other arithmetic, later_sum(): lax.all_to_all(shifted.astype(jnp.bfloat16), 'seq', split_axis=0, concat_...  7.82 us
    all_to_all x1, waiting for transfers between devices, earlier_sum(): lax.all_to_all(shifted.astype(jnp.bfloat16), 'seq', split_axis=0, concat_...  6.29 us
    all_to_all x2, other arithmetic, earlier_sum(): lax.all_to_all(shifted.astype(jnp.bfloat16), 'seq', split_axis=0, concat_...  6.02 us
    dot_general x1, matrix products, body(): jnp.einsum('hts,the->she', masked, d_acc, preferred_element_type=f32)  5.18 us
  transfers between devices with their start and end apart: 2, of which 1 were waited for; matrix products, arithmetic and copies ran while one was open for 24% of the time, Pallas kernels for 0%

commit v1 on v0

v1 whole, which is shorter than its diff:
```python
import functools

import jax
import jax.numpy as jnp
from jax import lax
from jax.experimental import pallas as pl
from jax.experimental.pallas import tpu as pltpu
from jax.sharding import PartitionSpec as P

DH = 128
EPS = 1e-06
F32 = jnp.float32
BF16 = jnp.bfloat16
WIRE_LOCAL = jnp.bfloat16
WIRE_PLANE = jnp.bfloat16


def dot(a, b, ca, cb):
    return lax.dot_general(a, b, (((ca,), (cb,)), ((), ())), preferred_element_type=F32)


def remote(src, dst, send_sem, recv_sem, device):
    return pltpu.make_async_remote_copy(
        src_ref=src,
        dst_ref=dst,
        send_sem=send_sem,
        recv_sem=recv_sem,
        device_id={"seq": device},
        device_id_type=pl.DeviceIdType.MESH,
    )


class Scan:
    def __init__(self, me, planes, members, share, forward, bufs):
        (self.mine, self.states, self.total, self.run, self.out2, self.in2, self.out3,
         self.result, self.s1, self.r1, self.s2, self.r2, self.s3, self.r3) = bufs
        self.planes, self.members, self.share, self.forward = planes, members, share, forward
        self.z, self.j = me // members, me % members
        self.zz = self.z if forward else planes - 1 - self.z
        self.levels = planes.bit_length() - 1

    def push(self, h, value):
        o, i = h // self.share, h % self.share

        @pl.when(o == self.j)
        def _():
            self.states[i, self.j] = value.astype(self.states.dtype)

        @pl.when(o != self.j)
        def _():
            self.mine[h] = value.astype(self.mine.dtype)
            remote(self.mine.at[h], self.states.at[i, self.j], self.s1.at[h],
                   self.r1.at[i, self.j], self.z * self.members + o).start()

    def plane_device(self, zz):
        z = zz if self.forward else self.planes - 1 - zz
        return z * self.members + self.j

    def sends(self, level):
        return (self.zz & ((2 << level) - 1)) == (1 << level) - 1

    def up(self, level, i, d):
        return remote(self.out2.at[level, i], self.in2.at[level, i], self.s2.at[level, d, i],
                      self.r2.at[level, i], self.plane_device(self.zz + 1 + d))

    def start_level(self, level, i):
        @pl.when(self.sends(level))
        def _():
            value = self.total[i] if level == 0 else self.run[i] + self.total[i]
            self.out2[level, i] = value.astype(self.out2.dtype)
            for d in range(1 << level):
                self.up(level, i, d).start()

    def gather(self):
        for i in range(self.share):
            for s in range(1, self.members):
                o = self.j ^ s
                remote(self.mine.at[0], self.states.at[i, o], self.s1.at[0], self.r1.at[i, o],
                       self.z * self.members + o).wait_recv()
            total = self.states[i, 0].astype(F32)
            for o in range(1, self.members):
                total += self.states[i, o].astype(F32)
            self.total[i] = total
            self.run[i] = jnp.zeros_like(total)
            self.start_level(0, i)

    def spread(self):
        for i in range(self.share):
            for level in range(self.levels):
                if level:
                    self.start_level(level, i)

                @pl.when(((self.zz >> level) & 1) == 1)
                def _():
                    self.up(level, i, 0).wait_recv()
                    self.run[i] += self.in2[level, i].astype(F32)

            total = self.run[i]
            order = range(self.members) if self.forward else range(self.members - 1, -1, -1)
            h = self.j * self.share + i
            for o in order:
                rounded = total.astype(BF16)
                total += self.states[i, o].astype(F32)

                @pl.when(o == self.j)
                def _():
                    self.result[h] = rounded

                @pl.when(o != self.j)
                def _():
                    self.out3[i, o] = rounded
                    remote(self.out3.at[i, o], self.result.at[h], self.s3.at[i, o],
                           self.r3.at[h], self.z * self.members + o).start()

    def take(self, h):
        o = h // self.share

        @pl.when(o != self.j)
        def _():
            remote(self.out3.at[0, 0], self.result.at[h], self.s3.at[0, 0], self.r3.at[h],
                   self.z * self.members + o).wait_recv()

    def drain(self):
        for i in range(self.share):
            for s in range(1, self.members):
                o = self.j ^ s
                h = o * self.share + i
                remote(self.mine.at[h], self.states.at[i, self.j], self.s1.at[h],
                       self.r1.at[i, self.j], self.z * self.members + o).wait_send()
                remote(self.out3.at[i, o], self.result.at[h], self.s3.at[i, o], self.r3.at[h],
                       self.z * self.members + o).wait_send()
            for level in range(self.levels):
                @pl.when(self.sends(level))
                def _():
                    for d in range(1 << level):
                        self.up(level, i, d).wait_send()


def kernel(n, members, q_hbm, k_hbm, v_hbm, g_hbm, relaid, dq_hbm, dk_hbm, dv_hbm,
           q_ref, k_ref, v_ref, g_ref, dq_ref, dk_ref, dv_ref, score, intra, out, d_acc,
           dk_part, dv_part, in_sem, out_sem, own_sem, relaid_send, relaid_recv, *scans):
    me = lax.axis_index("seq")
    rows, width = q_ref.shape
    heads = width // DH
    planes, share = n // members, heads // members
    pieces = n // heads
    piece = rows // pieces
    fwd = Scan(me, planes, members, share, True, scans[: len(scans) // 2])
    bwd = Scan(me, planes, members, share, False, scans[len(scans) // 2:])

    loads = [
        pltpu.make_async_copy(src, dst, in_sem.at[x])
        for x, (src, dst) in enumerate(
            ((k_hbm, k_ref), (v_hbm, v_ref), (q_hbm, q_ref), (g_hbm, g_ref)))
    ]
    for load in loads:
        load.start()
    barrier = pltpu.get_barrier_semaphore()

    def greet(s, carry):
        pl.semaphore_signal(barrier, inc=1, device_id={"seq": lax.rem(me + s, n)},
                            device_id_type=pl.DeviceIdType.MESH)
        return carry

    lax.fori_loop(1, n, greet, 0)

    def cols(h):
        return pl.ds(pl.multiple_of(h * DH, DH), DH)

    loads[0].wait()
    loads[1].wait()
    pl.semaphore_wait(barrier, n - 1)

    def local_step(t, carry):
        h = (fwd.j ^ (members - 1 - t % members)) * share + t // members
        fwd.push(h, dot(k_ref[:, cols(h)], v_ref[:, cols(h)], 0, 0))
        return carry

    lax.fori_loop(0, heads, local_step, 0)
    loads[2].wait()
    causal = (lax.broadcasted_iota(jnp.int32, (rows, rows), 0)
              >= lax.broadcasted_iota(jnp.int32, (rows, rows), 1))

    def intra_step(h, carry):
        s = dot(q_ref[:, cols(h)], k_ref[:, cols(h)], 1, 1)
        s = jnp.where(causal, s, 0.0).astype(BF16)
        score[h] = s
        intra[h] = dot(s, v_ref[:, cols(h)], 1, 0)
        return carry

    lax.fori_loop(0, heads, intra_step, 0)
    loads[3].wait()
    fwd.gather()
    fwd.spread()

    def relaid_copy(h, p):
        return remote(out.at[h, pl.ds(p * piece, piece)],
                      relaid.at[0, pl.ds(pl.multiple_of(me * piece, 16), piece)],
                      relaid_send, relaid_recv, p * heads + h)

    def own_copy(p):
        return pltpu.make_async_copy(
            out.at[me % heads, pl.ds(pl.multiple_of(p * piece, 16), piece)],
            relaid.at[0, pl.ds(pl.multiple_of(me * piece, 16), piece)], own_sem)

    def main_step(t, carry):
        h = (((me // members) % members) ^ (members - 1 - t % members)) * share + t // members
        fwd.take(h)
        q = q_ref[:, cols(h)]
        acc = intra[h] + dot(q, fwd.result[h], 1, 0)
        inv = lax.rsqrt(jnp.mean(acc * acc, axis=-1, keepdims=True) + EPS)
        unit = acc * inv
        out[h] = unit.astype(BF16)
        for p in range(pieces):
            @pl.when(p * heads + h != me)
            def _():
                relaid_copy(h, p).start()
        g = g_ref[:, cols(h)].astype(F32)
        inner = jnp.mean(g * unit, axis=-1, keepdims=True)
        da = ((g - unit * inner) * inv).astype(BF16)
        d_acc[h] = da
        bwd.push(h, dot(q, da, 0, 0))
        return carry

    lax.fori_loop(0, heads, main_step, 0)
    own_copy(me // heads).start()

    def grad_step(h, carry):
        q, k, v = q_ref[:, cols(h)], k_ref[:, cols(h)], v_ref[:, cols(h)]
        da = d_acc[h]
        ds = dot(da, v, 1, 1)
        ds = jnp.where(causal, ds, 0.0).astype(BF16)
        dq_ref[:, cols(h)] = (dot(ds, k, 1, 0) + dot(da, fwd.result[h], 1, 1)).astype(BF16)
        dk_part[h] = dot(ds, q, 0, 0)
        dv_part[h] = dot(score[h], da, 0, 0)
        return carry

    lax.fori_loop(0, heads, grad_step, 0)
    dq_out = pltpu.make_async_copy(dq_ref, dq_hbm, out_sem.at[0])
    dq_out.start()
    bwd.gather()
    bwd.spread()

    def last_step(t, carry):
        h = (t % members) * share + t // members
        bwd.take(h)
        later = bwd.result[h]
        dk_ref[:, cols(h)] = (dk_part[h] + dot(v_ref[:, cols(h)], later, 1, 1)).astype(BF16)
        dv_ref[:, cols(h)] = (dv_part[h] + dot(k_ref[:, cols(h)], later, 1, 0)).astype(BF16)
        return carry

    lax.fori_loop(0, heads, last_step, 0)
    dk_out = pltpu.make_async_copy(dk_ref, dk_hbm, out_sem.at[1])
    dv_out = pltpu.make_async_copy(dv_ref, dv_hbm, out_sem.at[2])
    dk_out.start()
    dv_out.start()
    fwd.drain()
    bwd.drain()
    own_copy(me // heads).wait()
    whole = relaid.at[0, pl.ds(0, (n - 1) * piece)]
    pltpu.make_async_copy(whole, whole, relaid_send).wait()
    pltpu.make_async_copy(whole, whole, relaid_recv).wait()
    dq_out.wait()
    dk_out.wait()
    dv_out.wait()


def body(queries, keys, values, out_grad):
    n = lax.axis_size("seq")
    rows, width = queries.shape
    heads = width // DH
    members = min(heads, n // 4 if n <= heads else n // 8)
    planes, share = n // members, heads // members
    levels = planes.bit_length() - 1
    piece = rows * heads // n
    dma = pltpu.SemaphoreType.DMA
    state = (DH, DH)
    scan = [
        pltpu.VMEM((heads,) + state, WIRE_LOCAL),
        pltpu.VMEM((share, members) + state, WIRE_LOCAL),
        pltpu.VMEM((share,) + state, F32),
        pltpu.VMEM((share,) + state, F32),
        pltpu.VMEM((levels, share) + state, WIRE_PLANE),
        pltpu.VMEM((levels, share) + state, WIRE_PLANE),
        pltpu.VMEM((share, members) + state, BF16),
        pltpu.VMEM((heads,) + state, BF16),
        dma((heads,)),
        dma((share, members)),
        dma((levels, 1 << (levels - 1), share)),
        dma((levels, share)),
        dma((share, members)),
        dma((heads,)),
    ]
    by_head = (heads, rows, DH)
    any_space = pl.BlockSpec(memory_space=pl.ANY)
    return pl.pallas_call(
        functools.partial(kernel, n, members),
        out_shape=(
            jax.ShapeDtypeStruct((1, n * piece, DH), BF16),
            jax.ShapeDtypeStruct((rows, width), BF16),
            jax.ShapeDtypeStruct((rows, width), BF16),
            jax.ShapeDtypeStruct((rows, width), BF16),
        ),
        in_specs=[any_space] * 4,
        out_specs=(any_space,) * 4,
        scratch_shapes=[pltpu.VMEM((rows, width), BF16)] * 7
        + [
            pltpu.VMEM((heads, rows, rows), BF16),
            pltpu.VMEM(by_head, F32),
            pltpu.VMEM(by_head, BF16),
            pltpu.VMEM(by_head, BF16),
            pltpu.VMEM(by_head, F32),
            pltpu.VMEM(by_head, F32),
            dma((4,)),
            dma((3,)),
            dma,
            dma,
            dma,
        ]
        + scan
        + scan,
        compiler_params=pltpu.CompilerParams(
            collective_id=0, has_side_effects=True, vmem_limit_bytes=56 * 2**20
        ),
        cost_estimate=pl.CostEstimate(
            flops=heads * rows * DH * 12 * (rows + DH),
            bytes_accessed=8 * rows * width * 2,
            transcendentals=rows * heads,
        ),
    )(queries, keys, values, out_grad)


def solution(mesh):
    return jax.shard_map(
        body,
        mesh=mesh,
        in_specs=(P(("groups", "seq"), None),) * 4,
        out_specs=(P("seq", "groups", None),) + (P(("groups", "seq"), None),) * 3,
        check_vma=False,
    )
```

time: 184 us -> 90.5 us (0.49)
  Pallas kernels: 0 us -> 81.8 us
  blocking collectives: 80.5 us -> 0 us
  matrix products: 32.4 us -> 0 us
  local copies, waits for them, and re-layouts: 36.6 us -> 7.87 us
  other arithmetic: 16.5 us -> 0 us
  starting transfers between devices: 9.68 us -> 0 us
  waiting for transfers between devices: 6.29 us -> 0 us
    pallas_call x0 -> x1, Pallas kernels: none -> 81.8 us  [body(): pl.pallas_call(functools.partial(kernel, n, members), out_shape=(jax.Shap...]
    all_to_all x3 -> x0, blocking collectives: 80.5 us -> none  [the longest x1 32 us: earlier_sum(): lax.all_to_all(flat, 'seq', split_axis=1, concat_axis=0, tiled=True)]
    dot_general x14 -> x0, matrix products: 32.4 us -> none  [the longest x1 5.18 us: body(): jnp.einsum('hts,the->she', masked, d_acc, preferred_element_type=f32)]
    unnamed x36 -> x10, local copies, waits for them, and re-layouts: 25.7 us -> 7.87 us
    all_to_all x4 -> x0, other arithmetic: 13.8 us -> none  [the longest x2 7.82 us: later_sum(): lax.all_to_all(shifted.astype(jnp.bfloat16), 'seq', split_axis=0, concat_...]
    all_to_all x2 -> x0, starting transfers between devices: 9.68 us -> none  [the longest x1 5.06 us: earlier_sum(): lax.all_to_all(shifted.astype(jnp.bfloat16), 'seq', split_axis=0, concat_...]
    all_to_all x2 -> x0, waiting for transfers between devices: 6.29 us -> none  [the longest x1 6.29 us: earlier_sum(): lax.all_to_all(shifted.astype(jnp.bfloat16), 'seq', split_axis=0, concat_...]
    convert_element_type x1 -> x0, local copies, waits for them, and re-layouts: 3.2 us -> none  [body(): grad_rows = out_grad.reshape(rows, heads, DH).astype(f32)]
  transfers between devices with their start and end apart: 2 -> 0, of which waited for: 1 -> 0; matrix products, arithmetic and copies ran while one was open for 24% -> 0% of each run, Pallas kernels for 0% -> 0%
where the time goes in v1:
time: 90.5 us; the launch traced here: 90.3 us
  Pallas kernels  81.8 us (90%)
  local copies, waits for them, and re-layouts  7.87 us (9%)
    pallas_call x1, Pallas kernels, body(): pl.pallas_call(functools.partial(kernel, n, members), out_shape=(jax.Shap...  81.8 us
    unnamed x10, local copies, waits for them, and re-layouts  7.87 us

profile of v1, /device:TPU:0, one launch (start us, length us, event | category | flops | bytes accessed | tf_op | source)
XLA Modules:
  0.0 90.3 jit_solution(16456541976207007882)
XLA Ops:
  0.6 81.8 %shard_map.75 = (bf16[1,6144,128]{2,1,0:T(8,128)(2,1)}, bf16[384,2048]{1,0:T(8,128)(2,1)}, bf16[384,2048]{1,0:T(8,128)(2,1)}, bf16[384,2048]{1,0:T(8,128)(2,1)}) custom-call(bf16[384,2048]{1,0:T(8,128)(2,1)} %q_hbm.1, bf16[384,2048]{1,0:T(8,128)(2,1)} %k_hbm.1, bf16[384,2048]{1,0:T(8,128)(2,1)} %v_hbm.1, bf16[384,2048]{1,0:T(8,128)(2,1)} %g_hbm.1), custom_call_target="tpu_custom_call" | custom-call | flops 4831838208 | bytes 12582912 | tf_op jit(solution)/shard_map/pallas_call | solution.py:296
  82.4 0.0 copy-start.2
  82.5 2.8 %copy.12 = bf16[1,6144,128]{2,1,0:T(8,128)(2,1)} copy(bf16[1,6144,128]{2,1,0:T(8,128)(2,1)} %get-tuple-element.8) | data formatting | bytes 3145728
  85.2 0.0 copy-done.2
  85.2 0.0 copy-start.1
  85.2 1.1 %copy.13 = bf16[384,2048]{1,0:T(8,128)(2,1)} copy(bf16[384,2048]{1,0:T(8,128)(2,1)S(1)} %copy-done.2) | data formatting | bytes 3145728
  86.4 0.8 copy-done.1
  87.2 0.0 copy-start
  87.2 1.1 %copy.14 = bf16[384,2048]{1,0:T(8,128)(2,1)} copy(bf16[384,2048]{1,0:T(8,128)(2,1)S(1)} %copy-done.1) | data formatting | bytes 3145728
  88.3 0.8 copy-done
  89.2 1.1 %copy.15 = bf16[384,2048]{1,0:T(8,128)(2,1)} copy(bf16[384,2048]{1,0:T(8,128)(2,1)S(1)} %copy-done) | data formatting | bytes 3145728
Async XLA Ops:
  82.4 2.8 %copy-start.2 = (bf16[384,2048]{1,0:T(8,128)(2,1)S(1)}, bf16[384,2048]{1,0:T(8,128)(2,1)}, u32[]{:S(2)}) copy-start(bf16[384,2048]{1,0:T(8,128)(2,1)} %get-tuple-element.9) | copy-start | bytes 4718596
  85.2 2.0 %copy-start.1 = (bf16[384,2048]{1,0:T(8,128)(2,1)S(1)}, bf16[384,2048]{1,0:T(8,128)(2,1)}, u32[]{:S(2)}) copy-start(bf16[384,2048]{1,0:T(8,128)(2,1)} %get-tuple-element.10) | copy-start | bytes 4718596
  87.2 2.0 %copy-start = (bf16[384,2048]{1,0:T(8,128)(2,1)S(1)}, bf16[384,2048]{1,0:T(8,128)(2,1)}, u32[]{:S(2)}) copy-start(bf16[384,2048]{1,0:T(8,128)(2,1)} %get-tuple-element.11) | copy-start | bytes 4718596

commit v2 on v1

--- a/solution.py
+++ b/solution.py
@@ -13,6 +13,8 @@
 BF16 = jnp.bfloat16
 WIRE_LOCAL = jnp.bfloat16
 WIRE_PLANE = jnp.bfloat16
+UNROLL = 4
+CHUNKS = 4
 
 
 def dot(a, b, ca, cb):
@@ -39,16 +41,14 @@
         self.zz = self.z if forward else planes - 1 - self.z
         self.levels = planes.bit_length() - 1
 
-    def push(self, h, value):
+    def keep(self, h, value):
+        self.mine[h] = value.astype(self.mine.dtype)
+
+    def push(self, h):
         o, i = h // self.share, h % self.share
-
-        @pl.when(o == self.j)
-        def _():
-            self.states[i, self.j] = value.astype(self.states.dtype)
 
         @pl.when(o != self.j)
         def _():
-            self.mine[h] = value.astype(self.mine.dtype)
             remote(self.mine.at[h], self.states.at[i, self.j], self.s1.at[h],
                    self.r1.at[i, self.j], self.z * self.members + o).start()
 
@@ -77,6 +77,7 @@
                 o = self.j ^ s
                 remote(self.mine.at[0], self.states.at[i, o], self.s1.at[0], self.r1.at[i, o],
                        self.z * self.members + o).wait_recv()
+            self.states[i, self.j] = self.mine[self.j * self.share + i]
             total = self.states[i, 0].astype(F32)
             for o in range(1, self.members):
                 total += self.states[i, o].astype(F32)
@@ -171,12 +172,19 @@
     loads[1].wait()
     pl.semaphore_wait(barrier, n - 1)
 
-    def local_step(t, carry):
-        h = (fwd.j ^ (members - 1 - t % members)) * share + t // members
-        fwd.push(h, dot(k_ref[:, cols(h)], v_ref[:, cols(h)], 0, 0))
-        return carry
-
-    lax.fori_loop(0, heads, local_step, 0)
+    def in_order(first, step):
+        ts = [step * UNROLL + x for x in range(UNROLL)]
+        return [(first ^ (members - 1 - t % members)) * share + t // members for t in ts]
+
+    def local_step(step, carry):
+        hs = in_order(fwd.j, step)
+        for h in hs:
+            fwd.keep(h, dot(k_ref[:, cols(h)], v_ref[:, cols(h)], 0, 0))
+        for h in hs:
+            fwd.push(h)
+        return carry
+
+    lax.fori_loop(0, heads // UNROLL, local_step, 0)
     loads[2].wait()
     causal = (lax.broadcasted_iota(jnp.int32, (rows, rows), 0)
               >= lax.broadcasted_iota(jnp.int32, (rows, rows), 1))
@@ -188,7 +196,7 @@
         intra[h] = dot(s, v_ref[:, cols(h)], 1, 0)
         return carry
 
-    lax.fori_loop(0, heads, intra_step, 0)
+    lax.fori_loop(0, heads, intra_step, 0, unroll=UNROLL)
     loads[3].wait()
     fwd.gather()
     fwd.spread()
@@ -203,26 +211,30 @@
             out.at[me % heads, pl.ds(pl.multiple_of(p * piece, 16), piece)],
             relaid.at[0, pl.ds(pl.multiple_of(me * piece, 16), piece)], own_sem)
 
-    def main_step(t, carry):
-        h = (((me // members) % members) ^ (members - 1 - t % members)) * share + t // members
-        fwd.take(h)
-        q = q_ref[:, cols(h)]
-        acc = intra[h] + dot(q, fwd.result[h], 1, 0)
-        inv = lax.rsqrt(jnp.mean(acc * acc, axis=-1, keepdims=True) + EPS)
-        unit = acc * inv
-        out[h] = unit.astype(BF16)
-        for p in range(pieces):
-            @pl.when(p * heads + h != me)
-            def _():
-                relaid_copy(h, p).start()
-        g = g_ref[:, cols(h)].astype(F32)
-        inner = jnp.mean(g * unit, axis=-1, keepdims=True)
-        da = ((g - unit * inner) * inv).astype(BF16)
-        d_acc[h] = da
-        bwd.push(h, dot(q, da, 0, 0))
-        return carry
-
-    lax.fori_loop(0, heads, main_step, 0)
+    def main_step(step, carry):
+        hs = in_order((me // members) % members, step)
+        for h in hs:
+            fwd.take(h)
+        for h in hs:
+            q = q_ref[:, cols(h)]
+            acc = intra[h] + dot(q, fwd.result[h], 1, 0)
+            inv = lax.rsqrt(jnp.mean(acc * acc, axis=-1, keepdims=True) + EPS)
+            unit = acc * inv
+            out[h] = unit.astype(BF16)
+            g = g_ref[:, cols(h)].astype(F32)
+            inner = jnp.mean(g * unit, axis=-1, keepdims=True)
+            da = ((g - unit * inner) * inv).astype(BF16)
+            d_acc[h] = da
+            bwd.keep(h, dot(q, da, 0, 0))
+        for h in hs:
+            for p in range(pieces):
+                @pl.when(p * heads + h != me)
+                def _():
+                    relaid_copy(h, p).start()
+            bwd.push(h)
+        return carry
+
+    lax.fori_loop(0, heads // UNROLL, main_step, 0)
     own_copy(me // heads).start()
 
     def grad_step(h, carry):
@@ -235,21 +247,25 @@
         dv_part[h] = dot(score[h], da, 0, 0)
         return carry
 
-    lax.fori_loop(0, heads, grad_step, 0)
+    lax.fori_loop(0, heads, grad_step, 0, unroll=UNROLL)
     dq_out = pltpu.make_async_copy(dq_ref, dq_hbm, out_sem.at[0])
     dq_out.start()
     bwd.gather()
     bwd.spread()
 
-    def last_step(t, carry):
-        h = (t % members) * share + t // members
-        bwd.take(h)
-        later = bwd.result[h]
-        dk_ref[:, cols(h)] = (dk_part[h] + dot(v_ref[:, cols(h)], later, 1, 1)).astype(BF16)
-        dv_ref[:, cols(h)] = (dv_part[h] + dot(k_ref[:, cols(h)], later, 1, 0)).astype(BF16)
-        return carry
-
-    lax.fori_loop(0, heads, last_step, 0)
+    def last_step(step, carry):
+        hs = in_order(0, step)
+        for h in hs:
+            bwd.take(h)
+        for h in hs:
+            later = bwd.result[h]
+            dk = dk_part[h] + dot(v_ref[:, cols(h)], later, 1, 1)
+            dv = dv_part[h] + dot(k_ref[:, cols(h)], later, 1, 0)
+            dk_ref[:, cols(h)] = dk.astype(BF16)
+            dv_ref[:, cols(h)] = dv.astype(BF16)
+        return carry
+
+    lax.fori_loop(0, heads // UNROLL, last_step, 0)
     dk_out = pltpu.make_async_copy(dk_ref, dk_hbm, out_sem.at[1])
     dv_out = pltpu.make_async_copy(dv_ref, dv_hbm, out_sem.at[2])
     dk_out.start()
@@ -263,6 +279,26 @@
     dq_out.wait()
     dk_out.wait()
     dv_out.wait()
+
+
+def place(*refs):
+    count = (len(refs) - 2) // 3
+    srcs, dsts, held = refs[:count], refs[count : 2 * count], refs[2 * count : 3 * count]
+    in_sem, out_sem = refs[-2:]
+    loads, stores = [], []
+    for x, (src, dst, buf) in enumerate(zip(srcs, dsts, held)):
+        size = src.shape[0] // CHUNKS
+        for c in range(CHUNKS):
+            part = pl.ds(c * size, size)
+            loads.append(pltpu.make_async_copy(src.at[part], buf.at[part], in_sem.at[x, c]))
+            stores.append(pltpu.make_async_copy(buf.at[part], dst.at[part], out_sem.at[x, c]))
+    for load in loads:
+        load.start()
+    for load, store in zip(loads, stores):
+        load.wait()
+        store.start()
+    for store in stores:
+        store.wait()
 
 
 def body(queries, keys, values, out_grad):
@@ -293,7 +329,7 @@
     ]
     by_head = (heads, rows, DH)
     any_space = pl.BlockSpec(memory_space=pl.ANY)
-    return pl.pallas_call(
+    found = pl.pallas_call(
         functools.partial(kernel, n, members),
         out_shape=(
             jax.ShapeDtypeStruct((1, n * piece, DH), BF16),
@@ -328,6 +364,20 @@
             transcendentals=rows * heads,
         ),
     )(queries, keys, values, out_grad)
+    flat = [x.reshape(-1, x.shape[-1]) for x in found]
+    placed = pl.pallas_call(
+        place,
+        out_shape=tuple(jax.ShapeDtypeStruct(x.shape, x.dtype) for x in flat),
+        in_specs=[any_space] * 4,
+        out_specs=(any_space,) * 4,
+        scratch_shapes=[pltpu.VMEM(x.shape, x.dtype) for x in flat]
+        + [dma((len(flat), CHUNKS))] * 2,
+        compiler_params=pltpu.CompilerParams(vmem_limit_bytes=56 * 2**20),
+        cost_estimate=pl.CostEstimate(
+            flops=0, bytes_accessed=16 * rows * width, transcendentals=0
+        ),
+    )(*flat)
+    return (placed[0][None],) + tuple(placed[1:])
 
 
 def solution(mesh):

time: 90.5 us -> 78.4 us (0.87)
  local copies, waits for them, and re-layouts: 7.87 us -> 0 us
  Pallas kernels: 81.8 us -> 77.7 us
    pallas_call x1, Pallas kernels: 81.8 us -> 72.2 us  [body(): pl.pallas_call(functools.partial(kernel, n, members), out_shape=(jax.Shap...]
    unnamed x10 -> x0, local copies, waits for them, and re-layouts: 7.87 us -> none
    pallas_call x0 -> x1, Pallas kernels: none -> 5.48 us  [body(): pl.pallas_call(place, out_shape=tuple((jax.ShapeDtypeStruct(x.shape, x.dt...]
where the time goes in v2:
time: 78.4 us; the launch traced here: 78.3 us
  Pallas kernels  77.7 us (99%)
    pallas_call x1, Pallas kernels, body(): pl.pallas_call(functools.partial(kernel, n, members), out_shape=(jax.Shap...  72.2 us
    pallas_call x1, Pallas kernels, body(): pl.pallas_call(place, out_shape=tuple((jax.ShapeDtypeStruct(x.shape, x.dt...  5.48 us

profile of v2, /device:TPU:0, one launch (start us, length us, event | category | flops | bytes accessed | tf_op | source)
XLA Modules:
  0.0 78.3 jit_solution(11855787157323534035)
XLA Ops:
  0.6 72.2 %shard_map.75 = (bf16[1,6144,128]{2,1,0:T(8,128)(2,1)}, bf16[384,2048]{1,0:T(8,128)(2,1)}, bf16[384,2048]{1,0:T(8,128)(2,1)}, bf16[384,2048]{1,0:T(8,128)(2,1)}) custom-call(bf16[384,2048]{1,0:T(8,128)(2,1)} %q_hbm.1, bf16[384,2048]{1,0:T(8,128)(2,1)} %k_hbm.1, bf16[384,2048]{1,0:T(8,128)(2,1)} %v_hbm.1, bf16[384,2048]{1,0:T(8,128)(2,1)} %g_hbm.1), custom_call_target="tpu_custom_call" | custom-call | flops 4831838208 | bytes 12582912 | tf_op jit(solution)/shard_map/pallas_call | solution.py:332
  72.8 5.5 %shard_map.76 = (bf16[6144,128]{1,0:T(8,128)(2,1)}, bf16[384,2048]{1,0:T(8,128)(2,1)}, bf16[384,2048]{1,0:T(8,128)(2,1)}, bf16[384,2048]{1,0:T(8,128)(2,1)}) custom-call(bf16[6144,128]{1,0:T(8,128)(2,1)} %bitcast.2, bf16[384,2048]{1,0:T(8,128)(2,1)} %get-tuple-element.13.refs_1_, bf16[384,2048]{1,0:T(8,128)(2,1)} %get-tuple-element.14.refs_2_, ...), custom_call_target="tpu_custom_call" | custom-call | bytes 12582912 | tf_op jit(solution)/shard_map/pallas_call | solution.py:368

commit v3 on v2

--- a/solution.py
+++ b/solution.py
@@ -196,7 +196,7 @@
         intra[h] = dot(s, v_ref[:, cols(h)], 1, 0)
         return carry
 
-    lax.fori_loop(0, heads, intra_step, 0, unroll=UNROLL)
+    lax.fori_loop(0, heads, intra_step, 0, unroll=2 * UNROLL)
     loads[3].wait()
     fwd.gather()
     fwd.spread()
@@ -247,7 +247,7 @@
         dv_part[h] = dot(score[h], da, 0, 0)
         return carry
 
-    lax.fori_loop(0, heads, grad_step, 0, unroll=UNROLL)
+    lax.fori_loop(0, heads, grad_step, 0, unroll=2 * UNROLL)
     dq_out = pltpu.make_async_copy(dq_ref, dq_hbm, out_sem.at[0])
     dq_out.start()
     bwd.gather()

time: 78.4 us -> 77.3 us (0.986)
  Pallas kernels: 77.7 us -> 76.5 us
    pallas_call x1, Pallas kernels: 72.2 us -> 71.1 us  [body(): pl.pallas_call(functools.partial(kernel, n, members), out_shape=(jax.Shap...]
where the time goes in v3:
time: 77.3 us; the launch traced here: 77.2 us
  Pallas kernels  76.5 us (99%)
    pallas_call x1, Pallas kernels, body(): pl.pallas_call(functools.partial(kernel, n, members), out_shape=(jax.Shap...  71.1 us
    pallas_call x1, Pallas kernels, body(): pl.pallas_call(place, out_shape=tuple((jax.ShapeDtypeStruct(x.shape, x.dt...  5.48 us

profile of v3, /device:TPU:0, one launch (start us, length us, event | category | flops | bytes accessed | tf_op | source)
XLA Modules:
  0.0 77.2 jit_solution(1062008451367514100)
XLA Ops:
  0.6 71.1 %shard_map.75 = (bf16[1,6144,128]{2,1,0:T(8,128)(2,1)}, bf16[384,2048]{1,0:T(8,128)(2,1)}, bf16[384,2048]{1,0:T(8,128)(2,1)}, bf16[384,2048]{1,0:T(8,128)(2,1)}) custom-call(bf16[384,2048]{1,0:T(8,128)(2,1)} %q_hbm.1, bf16[384,2048]{1,0:T(8,128)(2,1)} %k_hbm.1, bf16[384,2048]{1,0:T(8,128)(2,1)} %v_hbm.1, bf16[384,2048]{1,0:T(8,128)(2,1)} %g_hbm.1), custom_call_target="tpu_custom_call" | custom-call | flops 4831838208 | bytes 12582912 | tf_op jit(solution)/shard_map/pallas_call | solution.py:332
  71.7 5.5 %shard_map.76 = (bf16[6144,128]{1,0:T(8,128)(2,1)}, bf16[384,2048]{1,0:T(8,128)(2,1)}, bf16[384,2048]{1,0:T(8,128)(2,1)}, bf16[384,2048]{1,0:T(8,128)(2,1)}) custom-call(bf16[6144,128]{1,0:T(8,128)(2,1)} %bitcast.2, bf16[384,2048]{1,0:T(8,128)(2,1)} %get-tuple-element.13.refs_1_, bf16[384,2048]{1,0:T(8,128)(2,1)} %get-tuple-element.14.refs_2_, ...), custom_call_target="tpu_custom_call" | custom-call | bytes 12582912 | tf_op jit(solution)/shard_map/pallas_call | solution.py:368
